TPU v7x, 32 devices: a whole 2x2x4 slice. The times are simulated.
32 devices in a mesh: tgt: 8 (over y, x, core), grp: 4 (over z).
Axes of the slice: x: 2, y: 2, z: 4, core: 2. Of those that a mesh axis runs over, the one named last changes fastest.
Arguments:
- targets: bfloat16 [8, 64, 64, 128], P('tgt', 'grp'), may hold values from -6 to 6
- partners: bfloat16 [8, 64, 64, 128], P('tgt'), may hold values from -6 to 6
- occupations: float32 [8], replicated, may hold values from 0.2 to 2
- slot_partner: int32 [8], replicated, may hold values from 0 to 7, each once
- screening: float32 [1], replicated, may hold values from 0.3 to 0.6
Outputs:
- exchange: float32 [8, 64, 64, 128], P('tgt', 'grp')
Inputs may be any that keep to these rules, and one draw needn't show every extreme that they name: `slot_partner`: every partner id appears in exactly one slot.
All inputs are finite; a program needn't handle non-finite values.
Results may differ from a plain program's by a relative error of at most 0.011.
Values may be sent and summed in bfloat16 or wider, within the bound.
A program may use at most 64 MiB of HBM per device.

v0:
```python
import math

import jax
import jax.numpy as jnp
from jax import lax
from jax.sharding import PartitionSpec as P

coulomb_scale = 0.1


def from_behind(value, axis, steps):
    count = lax.axis_size(axis)
    pairs = [(source, (source + steps) % count) for source in range(count)]
    return lax.ppermute(value, axis, pairs)


def fourier_table(points):
    indices = jnp.arange(points, dtype=jnp.int32)
    phases = indices[:, None] * indices[None, :] % points
    angles = phases.astype(jnp.float32) * (2.0 * math.pi / points)
    norm_factor = 1.0 / math.sqrt(points)
    return jnp.concatenate(
        [jnp.cos(angles) * norm_factor, jnp.sin(angles) * norm_factor], axis=0
    ).astype(jnp.bfloat16)


def coulomb_kernel(points, screening):
    indices = jnp.arange(points, dtype=jnp.int32)
    signed = jnp.where(indices < points // 2, indices, indices - points).astype(jnp.float32) * (
        2.0 * math.pi / points
    )
    squares = signed * signed
    wave_sq = squares[:, None, None] + squares[None, :, None] + squares[None, None, :]
    screen_wave = screening[0] * (2.0 * math.pi / points)
    inverse_sq = coulomb_scale / (wave_sq + screen_wave * screen_wave)
    return jnp.concatenate([inverse_sq, inverse_sq], axis=-1)


def slot_weights(occupations, slot_partner):
    ids = jnp.arange(occupations.shape[0], dtype=jnp.int32)
    match = slot_partner[:, None] == ids[None, :]
    return jnp.sum(jnp.where(match, occupations[None, :], 0.0), axis=1)


def last_axis_matrix(tables, orient):
    points = tables.shape[1]
    cosine = tables[:points].T
    sine_part = tables[points:].T
    upper_rows = jnp.concatenate([cosine, -orient * sine_part], axis=1)
    bottom = jnp.concatenate([orient * sine_part, cosine], axis=1)
    return jnp.concatenate([upper_rows, bottom], axis=0)


def combine(cos_part, sin_part, orient, points):
    real_part = cos_part[..., :points] + orient * sin_part[..., points:]
    imag_part = cos_part[..., points:] - orient * sin_part[..., :points]
    return jnp.concatenate([real_part, imag_part], axis=-1).astype(jnp.bfloat16)


def section_last(field, matrix):
    flat = field.reshape(-1, matrix.shape[0])
    result = jnp.dot(flat, matrix, preferred_element_type=jnp.float32)
    return result.reshape(field.shape).astype(jnp.bfloat16)


def section_middle(field, tables, orient):
    points = tables.shape[1]
    stacked = jnp.einsum("ky,bxyw->bxkw", tables, field, preferred_element_type=jnp.float32)
    return combine(stacked[:, :, :points], stacked[:, :, points:], orient, points)


def section_first(field, tables, orient):
    points = tables.shape[1]
    stacked = jnp.einsum("kx,bxyw->bkyw", tables, field, preferred_element_type=jnp.float32)
    return combine(stacked[:, :points], stacked[:, points:], orient, points)


def exchange_term(targets, partner, weight, tables, forward_matrix, inverse_matrix, kernel):
    points = tables.shape[1]
    part_real = partner[..., :points].astype(jnp.float32)
    part_imag = partner[..., points:].astype(jnp.float32)
    tgt_real = targets[..., :points].astype(jnp.float32)
    tgt_imag = targets[..., points:].astype(jnp.float32)
    density = jnp.concatenate(
        [part_real * tgt_real + part_imag * tgt_imag, part_real * tgt_imag - part_imag * tgt_real],
        axis=-1,
    ).astype(jnp.bfloat16)
    spectrum = section_first(
        section_middle(section_last(density, forward_matrix), tables, 1.0), tables, 1.0
    )
    scaled = (spectrum.astype(jnp.float32) * kernel).astype(jnp.bfloat16)
    potential = section_last(
        section_middle(section_first(scaled, tables, -1.0), tables, -1.0), inverse_matrix
    )
    pot_real = potential[..., :points].astype(jnp.float32)
    pot_imag = potential[..., points:].astype(jnp.float32)
    real_part = pot_real * part_real - pot_imag * part_imag
    imag_part = pot_real * part_imag + pot_imag * part_real
    return weight * jnp.concatenate([real_part, imag_part], axis=-1)


def body(targets, partners, occupations, slot_partner, screening):
    gathered = lax.all_gather(targets, "grp", axis=1, tiled=True)
    points = gathered.shape[1]
    tables = fourier_table(points)
    forward_matrix = last_axis_matrix(tables, 1.0)
    inverse_matrix = last_axis_matrix(tables, -1.0)
    kernel = coulomb_kernel(points, screening)
    slot_weight = slot_weights(occupations, slot_partner)
    tgt_count = lax.axis_size("tgt")
    grp_count = lax.axis_size("grp")
    rounds = tgt_count // grp_count
    group_index = lax.axis_index("grp")
    own_index = lax.axis_index("tgt")
    partner_local = partners[0]
    totals = jnp.zeros(gathered.shape, jnp.float32)
    current = partner_local
    for bit_index in range(grp_count.bit_length() - 1):
        shifted = from_behind(current, "tgt", rounds * (1 << bit_index))
        current = jnp.where((group_index >> bit_index) % 2 == 1, shifted, current)

    def neighbour_round(round_index, state_pair):
        running, holding = state_pair
        slot_index = (own_index - group_index * rounds - round_index) % tgt_count
        weight = lax.dynamic_slice_in_dim(slot_weight, slot_index, 1)[0]
        running = running + exchange_term(
            gathered, holding, weight, tables, forward_matrix, inverse_matrix, kernel
        )
        holding = from_behind(holding, "tgt", 1)
        return (running, holding)

    totals, current = lax.fori_loop(0, rounds - 1, neighbour_round, (totals, current))
    final_slot = (own_index - group_index * rounds - (rounds - 1)) % tgt_count
    weight = lax.dynamic_slice_in_dim(slot_weight, final_slot, 1)[0]
    totals = totals + exchange_term(
        gathered, current, weight, tables, forward_matrix, inverse_matrix, kernel
    )
    summed = lax.psum_scatter(
        totals.astype(jnp.bfloat16), "grp", scatter_dimension=1, tiled=True
    ).astype(jnp.float32)
    return -summed


def solution(mesh):
    in_specs = (P("tgt", "grp", None, None), P("tgt", None, None, None), P(), P(), P())
    out_specs = P("tgt", "grp", None, None)
    return jax.shard_map(body, mesh=mesh, in_specs=in_specs, out_specs=out_specs, check_vma=False)
```

profile of v0, /device:TPU:1, one launch (start us, length us, event | category | flops | bytes accessed | tf_op | source)
XLA Modules:
  0.0 167.1 jit_solution(14361035300398756644)
XLA Ops:
  6.5 2.0 %collective-permute-start = (bf16[64,64,128]{2,1,0:T(8,128)(2,1)}, bf16[64,64,128]{2,1,0:T(8,128)(2,1)S(1)}, u32[]{:S(2)}, u32[]{:S(2)}) collective-permute-start(bf16[64,64,128]{2,1,0:T(8,128)(2,1)} %bitcast.159), channel_id=1, source_target_pairs={{0,8},{4,12},{8,16},{12,20},{16,24},{20,28},{24,0},{28,4},{1,9},{5... | collective-permute-start | bytes 3145736 | tf_op jit(solution)/shard_map/ppermute | solution.py:14
  8.6 24.0 %collective-permute-done = bf16[64,64,128]{2,1,0:T(8,128)(2,1)S(1)} collective-permute-done((bf16[64,64,128]{2,1,0:T(8,128)(2,1)}, bf16[64,64,128]{2,1,0:T(8,128)(2,1)S(1)}, u32[]{:S(2)}, u32[]{:S(2)}) %collective-permute-start) | collective-permute-done | bytes 1048608 | tf_op jit(solution)/shard_map/ppermute | solution.py:14
  32.6 1.3 broadcast_select_fusion
  34.0 1.2 collective-permute-start.1
  35.2 0.1 fusion.103
  35.4 0.2 select_reduce_fusion
  35.6 22.0 %collective-permute-done.1 = bf16[64,64,128]{2,1,0:T(8,128)(2,1)S(1)} collective-permute-done((bf16[64,64,128]{2,1,0:T(8,128)(2,1)S(1)}, bf16[64,64,128]{2,1,0:T(8,128)(2,1)S(1)}, u32[]{:S(2)}, u32[]{:S(2)}) %collective-permute-start.1) | collective-permute-done | bytes 1048608 | tf_op jit(solution)/shard_map/ppermute | solution.py:14
  57.7 2.2 %collective-permute-start.2 = (bf16[64,64,128]{2,1,0:T(8,128)(2,1)S(1)}, bf16[64,64,128]{2,1,0:T(8,128)(2,1)}, u32[]{:S(2)}, u32[]{:S(2)}) collective-permute-start(bf16[64,64,128]{2,1,0:T(8,128)(2,1)S(1)} %broadcast_select_fusion.1), channel_id=1, source_target_pairs={{0,4},{4,8},{8,12},{12,16},{16,20},{20,24},{24,28},{28,0},{1,5},{5... | collective-permute-start | bytes 3145736 | tf_op jit(solution)/shard_map/while/body/eval_jaxpr/ppermute | solution.py:14
  60.5 0.6 fusion.117
  61.1 0.1 fusion.102
  61.3 0.1 broadcast_multiply_fusion
  61.4 0.2 multiply_convert_fusion.4
  61.8 0.6 add_divide_fusion
  62.4 1.3 all-gather.2.cloned.1.call-done
  63.7 7.9 %collective-permute-done.2 = bf16[64,64,128]{2,1,0:T(8,128)(2,1)} collective-permute-done((bf16[64,64,128]{2,1,0:T(8,128)(2,1)S(1)}, bf16[64,64,128]{2,1,0:T(8,128)(2,1)}, u32[]{:S(2)}, u32[]{:S(2)}) %collective-permute-start.2) | collective-permute-done | bytes 1048608 | tf_op jit(solution)/shard_map/while/body/eval_jaxpr/ppermute | solution.py:14
  71.6 5.4 %fusion.57 = (bf16[64,64,64]{2,1,0:T(8,128)(2,1)}, bf16[64,64,64]{2,1,0:T(8,128)(2,1)}, bf16[64,64,64]{2,1,0:T(8,128)(2,1)}, bf16[64,64,64]{2,1,0:T(8,128)(2,1)}) fusion(bf16[1,64,64,128]{3,2,1,0:T(8,128)(2,1)} %bitcast.158, bf16[64,64,128]{2,1,0:T(8,128)(2,1)} %collective-permute-done.2, bf16[64,64,128]{2,1,0:T(8,128)(2,1)S(1)} %broadcast_select_fusion.1), kind=kLoop, calls=%fused_computation.107 | loop fusion | flops 5767168 | bytes 5242880 | tf_op jit(solution)/shard_map/concatenate | solution.py:84
  77.0 4.7 %convolution_bitcast_fusion.2 = f32[1,64,128,128]{3,2,1,0:T(8,128)} fusion(bf16[128,64,1]{0,1,2:T(8,128)(2,1)S(1)} %maximum_bitcast_fusion, bf16[64,64,64]{2,1,0:T(8,128)(2,1)} %get-tuple-element.60, bf16[64,64,64]{2,1,0:T(8,128)(2,1)} %get-tuple-element.59, bf16[64,64]{1,0:T(8,128)(2,1)S(1)} %fusion.102, bf16[64,64]{1,0:T(8,128)(2,1)S(1)} %fusion.103, ...), kind=kOutput, calls=%fused_computation.20 | convolution fusion | flops 271187968 | bytes 5283840 | tf_op jit(solution)/shard_map/ky,bxyw->bxkw/dot_general | solution.py:68
  81.7 4.7 %fusion.48 = (bf16[64,64,64]{2,1,0:T(8,128)(2,1)S(1)}, bf16[64,64,64]{2,1,0:T(8,128)(2,1)S(1)}) fusion(f32[1,64,128,128]{3,2,1,0:T(8,128)} %convolution_bitcast_fusion.2), kind=kLoop, calls=%fused_computation.98 | loop fusion | flops 1048576 | bytes 5242880 | tf_op jit(solution)/shard_map/concatenate | solution.py:57
  86.3 0.6 pad_maximum_fusion.4
  86.9 0.9 convolution_bitcast_fusion.1
  87.8 1.2 fusion.50
  89.0 1.3 convolution_bitcast_fusion
  90.2 2.6 %fusion.52 = (bf16[64,64,64]{2,0,1:T(8,128)(2,1)}, bf16[64,64,64]{2,0,1:T(8,128)(2,1)}) fusion(f32[1,128,64,128]{3,1,2,0:T(8,128)S(1)} %convolution_bitcast_fusion), kind=kLoop, calls=%fused_computation.102 | loop fusion | flops 1572864 | bytes 5242880 | tf_op jit(solution)/shard_map/concatenate | solution.py:57
  92.8 4.7 %convolution_bitcast_fusion.5 = f32[1,64,128,128]{3,2,1,0:T(8,128)} fusion(bf16[128,64,1]{0,1,2:T(8,128)(2,1)S(1)} %maximum_bitcast_fusion, bf16[64,64,64]{2,1,0:T(8,128)(2,1)} %get-tuple-element.65, bf16[64,64,64]{2,1,0:T(8,128)(2,1)} %get-tuple-element.66, bf16[64,64]{1,0:T(8,128)(2,1)S(1)} %fusion.102, bf16[64,64]{1,0:T(8,128)(2,1)S(1)} %fusion.103, ...), kind=kOutput, calls=%fused_computation.23 | convolution fusion | flops 271187968 | bytes 5283840 | tf_op jit(solution)/shard_map/while/body/eval_jaxpr/ky,bxyw->bxkw/dot_general | solution.py:68
  97.5 4.7 %fusion.40 = (bf16[64,64,64]{2,1,0:T(8,128)(2,1)S(1)}, bf16[64,64,64]{2,1,0:T(8,128)(2,1)S(1)}) fusion(f32[1,64,128,128]{3,2,1,0:T(8,128)} %convolution_bitcast_fusion.5), kind=kLoop, calls=%fused_computation.90 | loop fusion | flops 1048576 | bytes 5242880 | tf_op jit(solution)/shard_map/while/body/eval_jaxpr/concatenate | solution.py:57
  102.1 0.6 pad_maximum_fusion.1
  102.7 0.9 convolution_bitcast_fusion.4
  103.6 1.4 fusion.42
  105.0 1.3 convolution_bitcast_fusion.3
  106.3 1.2 fusion.44
  107.5 0.6 pad_maximum_fusion.2
  108.1 0.9 fusion.83
  108.9 2.4 %copy.51 = f32[64,128,128]{1,0,2:T(8,128)S(1)} copy(f32[64,128,128]{1,2,0:T(8,128)S(1)} %fusion.83) | data formatting | bytes 8388608 | tf_op jit(solution)/shard_map/while/body/eval_jaxpr/ky,bxyw->bxkw/dot_general | solution.py:68
  111.4 1.2 fusion.46
  112.6 0.6 pad_maximum_fusion.3
  113.2 0.9 fusion.38
  114.0 1.1 fusion.4
  115.2 0.3 copy-done.1
  115.6 0.6 pad_maximum_fusion.5
  116.1 0.9 fusion.79
  117.0 2.7 %copy.50 = f32[64,128,128]{1,0,2:T(8,128)S(1)} copy(f32[64,128,128]{1,2,0:T(8,128)S(1)} %fusion.79) | data formatting | bytes 8388608 | tf_op jit(solution)/shard_map/ky,bxyw->bxkw/dot_general | solution.py:68
  119.7 1.2 fusion.54
  120.9 0.6 pad_maximum_fusion.6
  121.5 0.9 fusion.39
  122.4 2.6 %fusion.10 = (f32[1,64,64,64]{3,2,1,0:T(8,128)S(1)}, f32[1,64,64,64]{3,2,1,0:T(8,128)S(1)}) fusion(bf16[1,64,64,128]{3,2,1,0:T(8,128)(2,1)S(1)} %fusion.39, bf16[64,64,128]{2,1,0:T(8,128)(2,1)} %collective-permute-done.2), kind=kLoop, calls=%fused_computation.34 | loop fusion | flops 2621440 | bytes 4194304 | tf_op jit(solution)/shard_map/sub | solution.py:97
  125.0 3.3 %fusion.37 = bf16[1,64,64,128]{3,2,1,0:T(8,128)(2,1)} fusion(f32[1,64,64,64]{3,2,1,0:T(8,128)S(1)} %get-tuple-element.62, f32[1,64,64,64]{3,2,1,0:T(8,128)S(1)} %get-tuple-element.61, f32[1,64,64,64]{3,2,1,0:T(8,128)S(1)} %get-tuple-element.58, f32[1,64,64,64]{3,2,1,0:T(8,128)S(1)} %get-tuple-element.57, f32[]{:T(128)} %bitcast.38, f32[]{:T(128)} %bitcast), kind=kLoop, calls=%fused_computation.79 | loop fusion | flops 3145728 | bytes 5242888 | tf_op jit(solution)/shard_map/convert_element_type | solution.py:139
  128.3 30.1 %reduce-scatter.2.cloned.1.call-done = bf16[1,16,64,128]{3,2,1,0:T(8,128)(2,1)} async-done(((bf16[1,64,64,128]{3,2,1,0:T(8,128)(2,1)}), bf16[1,16,64,128]{3,2,1,0:T(8,128)(2,1)}) %reduce-scatter.2.cloned.1.call-update) | async-done | bytes 262160 | tf_op jit(solution)/shard_map/reduce_scatter | solution.py:138
  158.4 1.8 %convert_negate_fusion = f32[1,16,64,128]{3,2,1,0:T(8,128)} fusion(bf16[1,16,64,128]{3,2,1,0:T(8,128)(2,1)} %reduce-scatter.2.cloned.1.call-done), kind=kLoop, calls=%fused_computation.142 | loop fusion | flops 262144 | bytes 786432 | tf_op jit(solution)/shard_map/neg | solution.py:141
  (15 shorter events, 0.5 us)
Async XLA Ops:
  6.5 28.9 %copy-start.3 = (s32[8]{0:T(128)S(1)}, s32[8]{0:T(128)}, u32[]{:S(2)}) copy-start(s32[8]{0:T(128)} %param.8) | copy-start | bytes 100
  6.5 28.9 %copy-start.2 = (f32[8]{0:T(128)S(1)}, f32[8]{0:T(128)}, u32[]{:S(2)}) copy-start(f32[8]{0:T(128)} %param.7) | copy-start | bytes 100
  6.5 57.1 %all-gather.2.cloned.1.call-start = ((), (), s32[]{:S(2)}) async-start(), calls=%async_computation.1 | async-start | bytes 1310720 | tf_op jit(solution)/shard_map/all_gather | solution.py:103
  6.5 26.1 %collective-permute-start = (bf16[64,64,128]{2,1,0:T(8,128)(2,1)}, bf16[64,64,128]{2,1,0:T(8,128)(2,1)S(1)}, u32[]{:S(2)}, u32[]{:S(2)}) collective-permute-start(bf16[64,64,128]{2,1,0:T(8,128)(2,1)} %bitcast.159), channel_id=1, source_target_pairs={{0,8},{4,12},{8,16},{12,20},{16,24},{20,28},{24,0},{28,4},{1,9},{5... | collective-permute-start | bytes 3145736 | tf_op jit(solution)/shard_map/ppermute | solution.py:14
  34.0 23.6 %collective-permute-start.1 = (bf16[64,64,128]{2,1,0:T(8,128)(2,1)S(1)}, bf16[64,64,128]{2,1,0:T(8,128)(2,1)S(1)}, u32[]{:S(2)}, u32[]{:S(2)}) collective-permute-start(bf16[64,64,128]{2,1,0:T(8,128)(2,1)S(1)} %broadcast_select_fusion), channel_id=1, source_target_pairs={{0,16},{4,20},{8,24},{12,28},{16,0},{20,4},{24,8},{28,12},{1,17},{... | collective-permute-start | bytes 3145736 | tf_op jit(solution)/shard_map/ppermute | solution.py:14
  35.2 123.2 %reduce-scatter.2.cloned.1.call-start = ((), (), s32[]{:S(2)}) async-start(), calls=%async_computation.2 | async-start | bytes 1310720 | tf_op jit(solution)/shard_map/reduce_scatter | solution.py:138
  57.7 13.9 %collective-permute-start.2 = (bf16[64,64,128]{2,1,0:T(8,128)(2,1)S(1)}, bf16[64,64,128]{2,1,0:T(8,128)(2,1)}, u32[]{:S(2)}, u32[]{:S(2)}) collective-permute-start(bf16[64,64,128]{2,1,0:T(8,128)(2,1)S(1)} %broadcast_select_fusion.1), channel_id=1, source_target_pairs={{0,4},{4,8},{8,12},{12,16},{16,20},{20,24},{24,28},{28,0},{1,5},{5... | collective-permute-start | bytes 3145736 | tf_op jit(solution)/shard_map/while/body/eval_jaxpr/ppermute | solution.py:14
  114.0 1.2 copy-start
  114.0 1.5 copy-start.1
Sparse Core Ops, SparseCore 0:
  35.3 28.3 all-gather.1
  128.5 29.9 reduce-scatter.1
where the time goes:
time: 168 us; the launch traced here: 167 us
  waiting for transfers between devices  85.3 us (51%)
  other arithmetic  38.7 us (23%)
  matrix products  17.1 us (10%)
  between operations  14.3 us (9%)
  local copies, waits for them, and re-layouts  6.21 us (4%)
  starting transfers between devices  5.44 us (3%)
    ppermute x3, waiting for transfers between devices, from_behind(): return lax.ppermute(value, axis, pairs)  53.9 us
    reduce_scatter x1, waiting for transfers between devices, body(): lax.psum_scatter(totals.astype(jnp.bfloat16), 'grp', scatter_dimension=1,...  30.1 us
    concatenate x14, other arithmetic, combine(): return jnp.concatenate([real_part, imag_part], axis=-1).astype(jnp.bfloat16)  21.5 us
    dot_general x4, matrix products, section_middle(): jnp.einsum('ky,bxyw->bxkw', tables, field, preferred_element_type=jnp.flo...  11.1 us
    concatenate x1, other arithmetic, exchange_term(): jnp.concatenate([part_real * tgt_real + part_imag * tgt_imag, part_real *...  5.4 us
    ppermute x3, starting transfers between devices, from_behind(): return lax.ppermute(value, axis, pairs)  5.39 us
    dot_general x2, local copies, waits for them, and re-layouts, section_middle(): jnp.einsum('ky,bxyw->bxkw', tables, field, preferred_element_type=jnp.flo...  5.12 us
    dot_general x4, matrix products, section_first(): jnp.einsum('kx,bxyw->bkyw', tables, field, preferred_element_type=jnp.flo...  4.29 us
  transfers between devices with their start and end apart: 5, of which 5 were waited for; matrix products, arithmetic and copies ran while one was open for 1% of the time, Pallas kernels for 0%

commit v1 on v0

v1 whole, which is shorter than its diff:
```python
import functools
import math

import jax
import jax.numpy as jnp
import numpy as np
from jax import lax
from jax.experimental import pallas as pl
from jax.experimental.pallas import tpu as pltpu
from jax.sharding import PartitionSpec as P

coulomb_scale = 0.1
MESH = pl.DeviceIdType.MESH


def tables(points):
    indices = np.arange(points)
    angles = (indices[:, None] * indices[None, :] % points) * (2.0 * math.pi / points)
    norm = 1.0 / math.sqrt(points)
    bf16 = lambda a: a.astype(np.float32).astype(jnp.bfloat16).astype(np.float32)
    return bf16(np.cos(angles) * norm), bf16(np.sin(angles) * norm)


def matrices(points):
    c, s = tables(points)
    n = points
    fz = np.block([[c, -s], [s, c]])
    fz = np.concatenate([fz, fz[:, n:], -fz[:, :n]], axis=1)
    fy = np.block([[c, s], [-s, c]])
    iy = np.block([[c, -s], [s, c]])
    iz = np.block([[c, s], [-s, c]])
    iz = np.concatenate([iz, iz[:, n:], iz[:, :n]], axis=1)
    return [m.astype(jnp.bfloat16) for m in (fz, fy, iy, iz)]


def compute_kernel(n, tgt_ref, part_ref, fz_ref, fy_ref, iy_ref, iz_ref, occ_ref, slot_ref, scr_ref,
                   out_ref, s1, s2):
    f32, bf16 = jnp.float32, jnp.bfloat16
    R = tgt_ref.shape[0]
    w = 2 * n
    ld = s1.shape[0] // w
    G = 4
    weight = -occ_ref[slot_ref[lax.axis_index("tgt")]]
    unit = 2.0 * math.pi / n
    kappa = scr_ref[0] * unit
    kappa_sq = kappa * kappa
    signed = lambda i: jnp.where(i < n // 2, i, i - n).astype(f32) * unit
    lane = lax.broadcasted_iota(jnp.int32, (n, w), 1)
    gx = signed(lax.broadcasted_iota(jnp.int32, (n, w), 0))
    gz = signed(lane % n)
    base = gx * gx + gz * gz + kappa_sq
    low = lax.broadcasted_iota(jnp.int32, (G * n, w), 1) < n

    def dot(a, b):
        return jnp.dot(a, b, preferred_element_type=f32)

    def partner_parts(rows):
        q = part_ref[rows, :].astype(f32)
        turned = pltpu.roll(q, n, 1)
        return jnp.where(low, q, turned), jnp.where(low, -turned, q)

    for r in range(R):

        @pl.loop(0, n // G)
        def _(i):
            rows = pl.ds(pl.multiple_of(i * (G * n), G * n), G * n)
            t = tgt_ref[r, rows, :].astype(f32)
            q1, q2 = partner_parts(rows)
            density = (q1 * t - q2 * pltpu.roll(t, n, 1)).astype(bf16)
            f = dot(density, fz_ref[...]).astype(bf16)
            for a in range(0, G, 2):
                stack = [
                    jnp.concatenate([f[b * n:(b + 1) * n, :w], f[b * n:(b + 1) * n, w:]], axis=0)
                    for b in (a, a + 1)
                ]
                o = dot(fy_ref[...], jnp.concatenate(stack, axis=1))
                for b in range(2):
                    s1[pl.ds(i * G + a + b, w, stride=ld), :] = o[:, b * w:(b + 1) * w]

        @pl.loop(0, n // G)
        def _(i):
            for a in range(0, G, 2):
                stack, kern = [], []
                for b in range(2):
                    ky = i * G + a + b
                    top = s1[pl.ds(pl.multiple_of(ky * ld, 8), n), :]
                    bottom = s1[pl.ds(pl.multiple_of((ky + n) * ld, 8), n), :]
                    stack.append(jnp.concatenate([top, bottom], axis=0).astype(bf16))
                    gy = signed(ky)
                    k = coulomb_scale / (base + gy * gy)
                    kern.append(jnp.concatenate([k, k], axis=0))
                spectrum = dot(fy_ref[...], jnp.concatenate(stack, axis=1))
                scaled = (spectrum * jnp.concatenate(kern, axis=1)).astype(bf16)
                o = dot(iy_ref[...], scaled)
                for b in range(2):
                    s2[pl.ds(i * G + a + b, w, stride=ld), :] = o[:, b * w:(b + 1) * w]

        @pl.loop(0, n // G)
        def _(i):
            rows = pl.ds(pl.multiple_of(i * (G * n), G * n), G * n)
            parts = []
            for a in range(0, G, 2):
                stack = []
                for b in range(2):
                    x = i * G + a + b
                    top = s2[pl.ds(pl.multiple_of(x * ld, 8), n), :]
                    bottom = s2[pl.ds(pl.multiple_of((x + n) * ld, 8), n), :]
                    stack.append(jnp.concatenate([top, bottom], axis=0).astype(bf16))
                o = dot(iy_ref[:n, :], jnp.concatenate(stack, axis=1)).astype(bf16)
                parts += [o[:, :w], o[:, w:]]
            potential = dot(jnp.concatenate(parts, axis=0), iz_ref[...])
            q1, q2 = partner_parts(rows)
            out_ref[r, rows, :] = (
                weight * (potential[:, :w] * q1 + potential[:, w:] * q2)
            ).astype(bf16)


def gather_kernel(NT, NG, src, out, p1_send, p1_recv, p2_send, p2_recv, sib_send, sib_recv):
    R, C = NT // NG, NT // 2
    t, g = lax.axis_index("tgt"), lax.axis_index("grp")
    c, p = t // 2, t % 2
    own_set = t // R
    sibling = c * 2 + 1 - p
    inside = own_set == g

    barrier = pltpu.get_barrier_semaphore()
    for r in range(R):
        for h in range(NG):

            @pl.when(jnp.logical_not(inside & (t == g * R + r) & (h == g)))
            def _():
                pl.semaphore_signal(barrier, inc=1, device_id=(g * R + r, h), device_id_type=MESH)

    for m in range(1, C):
        pl.semaphore_signal(barrier, inc=1, device_id=((c + C - m) % C * 2 + p, g), device_id_type=MESH)
    pl.semaphore_signal(barrier, inc=1, device_id=(sibling, g), device_id_type=MESH)

    @pl.when(inside)
    def _():
        pl.semaphore_wait(barrier, NT - 1 + C)

    @pl.when(jnp.logical_not(inside))
    def _():
        pl.semaphore_wait(barrier, NT + C)

    def spread(j):
        return pltpu.make_async_remote_copy(
            src_ref=src.at[j], dst_ref=out.at[t % R, g, j], send_sem=p1_send.at[j],
            recv_sem=p1_recv.at[t % R, g], device_id=(j, own_set), device_id_type=MESH)

    def is_self(j):
        return inside & (t == j)

    own = pltpu.make_async_copy(src.at[t], out.at[t % R, g, t], p1_recv.at[t % R, g])
    for m in range(NT):
        j = (t + m) % NT
        if m == 0:

            @pl.when(inside)
            def _():
                own.start()

            @pl.when(jnp.logical_not(inside))
            def _():
                spread(j).start()
        else:
            spread(j).start()

    def peer(r, m):
        return pltpu.make_async_remote_copy(
            src_ref=out.at[r, :, t], dst_ref=out.at[r, :, t], send_sem=p2_send.at[r, m],
            recv_sem=p2_recv.at[r, m], device_id=((c + m) % C * 2 + p, g), device_id_type=MESH)

    def to_sibling(r, m):
        j = (c + C - m) % C * 2 + p
        return pltpu.make_async_remote_copy(
            src_ref=out.at[r, :, j], dst_ref=out.at[r, :, j], send_sem=sib_send.at[r, m],
            recv_sem=sib_recv.at[r, m], device_id=(sibling, g), device_id_type=MESH)

    for r in range(R):
        for h in range(NG):
            piece = out.at[r, h, t]
            pltpu.make_async_copy(piece, piece, p1_recv.at[r, h]).wait()
        for m in range(1, C):
            peer(r, m).start()
        to_sibling(r, 0).start()
    for r in range(R):
        for m in range(1, C):
            peer(r, m).wait_recv()
            to_sibling(r, m).start()
    for r in range(R):
        for m in range(C):
            to_sibling(r, m).wait()
            if m:
                peer(r, m).wait_send()
    for m in range(1, NT):
        spread((t + m) % NT).wait_send()

    @pl.when(jnp.logical_not(inside))
    def _():
        spread(t).wait_send()


def reduce_kernel(NT, NG, part, out, sib, acc, inbox, fin, final, s_send, s_recv, r_send, r_recv, f_send, f_recv):
    f32, bf16 = jnp.float32, jnp.bfloat16
    R, C = NT // NG, NT // 2
    t, g = lax.axis_index("tgt"), lax.axis_index("grp")
    c, p = t // 2, t % 2
    own_set = t // R
    sibling = c * 2 + 1 - p
    inside = own_set == g

    barrier = pltpu.get_barrier_semaphore()
    for m in range(NT):
        j = (t + m) % NT
        if m == 0:

            @pl.when(jnp.logical_not(inside))
            def _():
                pl.semaphore_signal(barrier, inc=1, device_id=(j, own_set), device_id_type=MESH)
        else:
            pl.semaphore_signal(barrier, inc=1, device_id=(j, own_set), device_id_type=MESH)
    for m in range(1, C):
        pl.semaphore_signal(barrier, inc=1, device_id=((c + C - m) % C * 2 + p, g), device_id_type=MESH)
    pl.semaphore_signal(barrier, inc=1, device_id=(sibling, g), device_id_type=MESH)

    @pl.when(inside)
    def _():
        pl.semaphore_wait(barrier, NT - 1 + C)

    @pl.when(jnp.logical_not(inside))
    def _():
        pl.semaphore_wait(barrier, NT + C)

    def to_sibling(r, m):
        d = (c + m) % C
        return pltpu.make_async_remote_copy(
            src_ref=part.at[r, :, d * 2 + 1 - p], dst_ref=sib.at[r, m], send_sem=s_send.at[r, m],
            recv_sem=s_recv.at[r, m], device_id=(sibling, g), device_id_type=MESH)

    def peer(r, m):
        return pltpu.make_async_remote_copy(
            src_ref=acc.at[r, m], dst_ref=inbox.at[r, m], send_sem=r_send.at[r, m],
            recv_sem=r_recv.at[r, m], device_id=((c + m) % C * 2 + p, g), device_id_type=MESH)

    def to_owner(r, h):
        return pltpu.make_async_remote_copy(
            src_ref=fin.at[r, h], dst_ref=final.at[t], send_sem=f_send.at[r, h],
            recv_sem=f_recv.at[t], device_id=(g * R + r, h), device_id_type=MESH)

    order = list(range(1, C)) + [0]
    for r in range(R):
        for m in order:
            to_sibling(r, m).start()
    for r in range(R):
        for m in order:
            to_sibling(r, m).wait_recv()
            mine = part[r, :, (c + m) % C * 2 + p]
            acc[r, m] = (mine.astype(f32) + sib[r, m].astype(f32)).astype(bf16)
            if m:
                peer(r, m).start()
    own = pltpu.make_async_copy(fin.at[t % R, g], final.at[t], f_recv.at[t])
    for r in range(R):
        for m in range(1, C):
            peer(r, m).wait_recv()
        total = acc[r, 0].astype(f32)
        for m in range(1, C):
            total = total + inbox[r, m].astype(f32)
        fin[r] = total.astype(bf16)
        for h in range(NG):
            here = inside & (t == g * R + r) & (g == h)

            @pl.when(here)
            def _():
                own.start()

            @pl.when(jnp.logical_not(here))
            def _():
                to_owner(r, h).start()

    for m in range(NT):
        j = (t + m) % NT
        piece = final.at[j]
        pltpu.make_async_copy(piece, piece, f_recv.at[j]).wait()
        out[j] = final[j].astype(f32)
    for r in range(R):
        for m in range(C):
            to_sibling(r, m).wait_send()
            if m:
                peer(r, m).wait_send()
        for h in range(NG):
            here = inside & (t == g * R + r) & (g == h)

            @pl.when(jnp.logical_not(here))
            def _():
                to_owner(r, h).wait_send()


def body(targets, partners, occupations, slot_partner, screening):
    NT, NG = lax.axis_size("tgt"), lax.axis_size("grp")
    R, C = NT // NG, NT // 2
    _, planes, n, w = targets.shape
    rows = planes * n // NT
    piece = (rows, w)
    vmem = pl.BlockSpec(memory_space=pltpu.VMEM)
    smem = pl.BlockSpec(memory_space=pltpu.SMEM)
    dma = pltpu.SemaphoreType.DMA
    bf16 = jnp.bfloat16
    limit = 48 << 20

    gathered = pl.pallas_call(
        functools.partial(gather_kernel, NT, NG),
        out_shape=jax.ShapeDtypeStruct((R, NG, NT) + piece, bf16),
        in_specs=[vmem],
        out_specs=vmem,
        scratch_shapes=[dma((NT,)), dma((R, NG)), dma((R, C)), dma((R, C)), dma((R, C)), dma((R, C))],
        compiler_params=pltpu.CompilerParams(
            collective_id=0, has_side_effects=True, vmem_limit_bytes=limit),
    )(targets.reshape((NT,) + piece))

    mats = [jnp.asarray(m) for m in matrices(n)]
    ld = n + 8
    partial = pl.pallas_call(
        functools.partial(compute_kernel, n),
        out_shape=jax.ShapeDtypeStruct((R, n * n, w), bf16),
        in_specs=[vmem] * 6 + [smem] * 3,
        out_specs=vmem,
        scratch_shapes=[pltpu.VMEM((w * ld, w), jnp.float32)] * 2,
        compiler_params=pltpu.CompilerParams(vmem_limit_bytes=limit),
    )(gathered.reshape(R, n * n, w), partners.reshape(n * n, w), *mats,
      occupations, slot_partner, screening)

    out = pl.pallas_call(
        functools.partial(reduce_kernel, NT, NG),
        out_shape=jax.ShapeDtypeStruct((NT,) + piece, jnp.float32),
        in_specs=[vmem],
        out_specs=vmem,
        scratch_shapes=[
            pltpu.VMEM((R, C, NG) + piece, bf16),
            pltpu.VMEM((R, C, NG) + piece, bf16),
            pltpu.VMEM((R, C, NG) + piece, bf16),
            pltpu.VMEM((R, NG) + piece, bf16),
            pltpu.VMEM((NT,) + piece, bf16),
            dma((R, C)), dma((R, C)), dma((R, C)), dma((R, C)), dma((R, NG)), dma((NT,)),
        ],
        compiler_params=pltpu.CompilerParams(
            collective_id=1, has_side_effects=True, vmem_limit_bytes=limit),
    )(partial.reshape((R, NG, NT) + piece))
    return out.reshape(targets.shape)


def solution(mesh):
    in_specs = (P("tgt", "grp", None, None), P("tgt", None, None, None), P(), P(), P())
    out_specs = P("tgt", "grp", None, None)
    return jax.shard_map(body, mesh=mesh, in_specs=in_specs, out_specs=out_specs, check_vma=False)
```

time: 168 us -> 98.2 us (0.58)
  Pallas kernels: 0 us -> 95 us
  waiting for transfers between devices: 85.3 us -> 0 us
  other arithmetic: 38.7 us -> 0 us
  matrix products: 17.1 us -> 0 us
  between operations: 14.3 us -> 0.85 us
  starting transfers between devices: 5.44 us -> 0 us
  local copies, waits for them, and re-layouts: 6.21 us -> 1.77 us
    pallas_call x0 -> x3, Pallas kernels: none -> 95 us  [the longest x1 37.5 us: body(): pl.pallas_call(functools.partial(gather_kernel, NT, NG), out_shape=jax.Sh...]
    ppermute x3 -> x0, waiting for transfers between devices: 53.9 us -> none  [from_behind(): return lax.ppermute(value, axis, pairs)]
    reduce_scatter x1 -> x0, waiting for transfers between devices: 30.1 us -> none  [body(): lax.psum_scatter(totals.astype(jnp.bfloat16), 'grp', scatter_dimension=1,...]
    concatenate x16 -> x0, other arithmetic: 27 us -> none  [the longest x14 21.5 us: combine(): return jnp.concatenate([real_part, imag_part], axis=-1).astype(jnp.bfloat16)]
    dot_general x10 -> x0, matrix products: 17.1 us -> none  [the longest x4 11.1 us: section_middle(): jnp.einsum('ky,bxyw->bxkw', tables, field, preferred_element_type=jnp.flo...]
    ppermute x3 -> x0, starting transfers between devices: 5.39 us -> none  [from_behind(): return lax.ppermute(value, axis, pairs)]
    dot_general x2 -> x0, local copies, waits for them, and re-layouts: 5.12 us -> none  [section_middle(): jnp.einsum('ky,bxyw->bxkw', tables, field, preferred_element_type=jnp.flo...]
    sub x2 -> x0, other arithmetic: 3.67 us -> none  [exchange_term(): real_part = pot_real * part_real - pot_imag * part_imag]
  transfers between devices with their start and end apart: 5 -> 0, of which waited for: 5 -> 0; matrix products, arithmetic and copies ran while one was open for 1% -> 0% of each run, Pallas kernels for 0% -> 0%
where the time goes in v1:
time: 98.2 us; the launch traced here: 97.6 us
  Pallas kernels  95 us (97%)
  local copies, waits for them, and re-layouts  1.77 us (2%)
    pallas_call x1, Pallas kernels, body(): pl.pallas_call(functools.partial(gather_kernel, NT, NG), out_shape=jax.Sh...  37.5 us
    pallas_call x1, Pallas kernels, body(): pl.pallas_call(functools.partial(compute_kernel, n), out_shape=jax.ShapeD...  34.9 us
    pallas_call x1, Pallas kernels, body(): pl.pallas_call(functools.partial(reduce_kernel, NT, NG), out_shape=jax.Sh...  22.7 us

profile of v1, /device:TPU:1, one launch (start us, length us, event | category | flops | bytes accessed | tf_op | source)
XLA Modules:
  0.0 97.6 jit_solution(17236954469922351993)
XLA Ops:
  0.0 0.0 copy-start
  0.7 0.0 copy-start.1
  0.8 0.9 copy-done.1
  1.7 0.0 copy-start.2
  1.7 0.0 copy-start.3
  1.7 0.0 copy-start.4
  1.7 0.0 copy-start.5
  1.7 0.0 copy-start.6
  1.7 0.0 copy-start.7
  1.7 37.5 %shard_map.91 = bf16[2,4,8,128,128]{4,3,2,1,0:T(8,128)(2,1)S(1)} custom-call(bf16[8,128,128]{2,1,0:T(8,128)(2,1)S(1)} %bitcast.9), custom_call_target="tpu_custom_call" | custom-call | tf_op jit(solution)/shard_map/pallas_call | solution.py:311
  39.2 0.0 copy-done
  39.2 0.0 copy-done.2
  39.2 0.0 copy-done.3
  39.2 0.0 copy-done.4
  39.2 0.0 copy-done.5
  39.2 0.0 copy-done.6
  39.2 0.0 copy-done.7
  39.3 34.9 %shard_map.92 = bf16[2,4096,128]{2,1,0:T(8,128)(2,1)S(1)} custom-call(bf16[2,4096,128]{2,1,0:T(8,128)(2,1)S(1)} %bitcast.6, bf16[4096,128]{1,0:T(8,128)(2,1)S(1)} %bitcast.8, bf16[128,256]{1,0:T(8,128)(2,1)S(1)} %copy-done.3, bf16[128,128]{1,0:T(8,128)(2,1)S(1)} %copy-done.5, bf16[128,128]{1,0:T(8,128)(2,1)S(1)} %copy-done.4, ...), custom_call_target="tpu_custom_call" | custom-call | tf_op jit(solution)/shard_map/pallas_call | solution.py:323
  74.2 22.7 %shard_map.93 = f32[8,128,128]{2,1,0:T(8,128)S(1)} custom-call(bf16[2,4,8,128,128]{4,3,2,1,0:T(8,128)(2,1)S(1)} %bitcast.5), custom_call_target="tpu_custom_call" | custom-call | tf_op jit(solution)/shard_map/pallas_call | solution.py:333
  96.8 0.8 copy.12
Async XLA Ops:
  0.0 39.2 %copy-start = (bf16[1,64,64,128]{3,2,1,0:T(8,128)(2,1)S(1)}, bf16[1,64,64,128]{3,2,1,0:T(8,128)(2,1)}, u32[]{:S(2)}) copy-start(bf16[1,64,64,128]{3,2,1,0:T(8,128)(2,1)} %param.10) | copy-start | bytes 3145732
  0.7 1.0 copy-start.1
  1.7 37.5 %copy-start.2 = (bf16[128,256]{1,0:T(8,128)(2,1)S(1)}, bf16[128,256]{1,0:T(8,128)(2,1)}, u32[]{:S(2)}) copy-start(bf16[128,256]{1,0:T(8,128)(2,1)} %constant.11.clone.iz_ref) | copy-start | bytes 196612
  1.7 37.5 %copy-start.3 = (bf16[128,256]{1,0:T(8,128)(2,1)S(1)}, bf16[128,256]{1,0:T(8,128)(2,1)}, u32[]{:S(2)}) copy-start(bf16[128,256]{1,0:T(8,128)(2,1)} %constant.8.clone.fz_ref) | copy-start | bytes 196612
  1.7 37.5 %copy-start.4 = (bf16[128,128]{1,0:T(8,128)(2,1)S(1)}, bf16[128,128]{1,0:T(8,128)(2,1)}, u32[]{:S(2)}) copy-start(bf16[128,128]{1,0:T(8,128)(2,1)} %constant.10.clone.iy_ref) | copy-start | bytes 98308
  1.7 37.5 %copy-start.5 = (bf16[128,128]{1,0:T(8,128)(2,1)S(1)}, bf16[128,128]{1,0:T(8,128)(2,1)}, u32[]{:S(2)}) copy-start(bf16[128,128]{1,0:T(8,128)(2,1)} %constant.9.clone.fy_ref) | copy-start | bytes 98308
  1.7 37.5 %copy-start.6 = (f32[8]{0:T(128)S(1)}, f32[8]{0:T(128)}, u32[]{:S(2)}) copy-start(f32[8]{0:T(128)} %occ_ref.1) | copy-start | bytes 100
  1.7 37.5 %copy-start.7 = (s32[8]{0:T(128)S(1)}, s32[8]{0:T(128)}, u32[]{:S(2)}) copy-start(s32[8]{0:T(128)} %slot_ref.1) | copy-start | bytes 100

commit v2 on v0

v2 whole, which is shorter than its diff:
```python
import functools
import math

import jax
import jax.numpy as jnp
import numpy as np
from jax import lax
from jax.experimental import pallas as pl
from jax.experimental.pallas import tpu as pltpu
from jax.sharding import PartitionSpec as P

coulomb_scale = 0.1
MESH = pl.DeviceIdType.MESH


def tables(points):
    indices = np.arange(points)
    angles = (indices[:, None] * indices[None, :] % points) * (2.0 * math.pi / points)
    norm = 1.0 / math.sqrt(points)
    bf16 = lambda a: a.astype(np.float32).astype(jnp.bfloat16).astype(np.float32)
    return bf16(np.cos(angles) * norm), bf16(np.sin(angles) * norm)


def matrices(points):
    c, s = tables(points)
    n = points
    fz = np.block([[c, -s], [s, c]])
    fz = np.concatenate([fz, fz[:, n:], -fz[:, :n]], axis=1)
    fy = np.block([[c, s], [-s, c]])
    iy = np.block([[c, -s], [s, c]])
    iz = np.block([[c, s], [-s, c]])
    iz = np.concatenate([iz, iz[:, n:], iz[:, :n]], axis=1)
    return [m.astype(jnp.bfloat16) for m in (fz, fy, iy, iz)]


def exchange_kernel(NT, NG, src, part_hbm, fz_ref, fy_ref, iy_ref, iz_ref, occ_ref, slot_ref, scr_ref, out,
                    gat, partner, q1_ref, q2_ref, kern_ref, s1, s2, part, sib, acc, inbox, fin, final,
                    load_sem, p1_send, p1_recv, p2_send, p2_recv, b_send, b_recv,
                    s_send, s_recv, r_send, r_recv, f_send, f_recv):
    f32, bf16 = jnp.float32, jnp.bfloat16
    R, C = NT // NG, NT // 2
    n = kern_ref.shape[0]
    w = 2 * n
    P2 = 2 * src.shape[1]
    k = P2 // n
    ld = s1.shape[0] // w
    t, g = lax.axis_index("tgt"), lax.axis_index("grp")
    c, p = t // 2, t % 2
    own_set = t // R
    sibling = c * 2 + 1 - p
    inside = own_set == g

    load = pltpu.make_async_copy(part_hbm, partner, load_sem)
    load.start()

    barrier = pltpu.get_barrier_semaphore()

    def greet(*device):
        pl.semaphore_signal(barrier, inc=1, device_id=device, device_id_type=MESH)

    for m in range(NT):
        if m == 0:
            pl.when(jnp.logical_not(inside))(lambda: greet(t, own_set))
        else:
            greet((t + m) % NT, own_set)
    for r in range(R):
        for h in range(NG):
            here = (t == g * R + r) & (g == h)
            pl.when(jnp.logical_not(here))(lambda: greet(g * R + r, h))
    for m in range(1, C):
        greet((c + m) % C * 2 + p, g)
    greet(sibling, g)

    @pl.when(inside)
    def _():
        pl.semaphore_wait(barrier, 2 * NT - 2 + C)

    @pl.when(jnp.logical_not(inside))
    def _():
        pl.semaphore_wait(barrier, 2 * NT + C)

    def remote(a, b, send, recv, *device):
        return pltpu.make_async_remote_copy(
            src_ref=a, dst_ref=b, send_sem=send, recv_sem=recv, device_id=device, device_id_type=MESH)

    def spread(j):
        return remote(src.at[j], gat.at[t % R, g, j // 2, j % 2], p1_send.at[j], p1_recv.at[t % R, g], j, own_set)

    own_piece = pltpu.make_async_copy(src.at[t], gat.at[t % R, g, c, p], p1_recv.at[t % R, g])
    for m in range(1, NT):
        spread((t + m) % NT).start()
    pl.when(inside)(own_piece.start)
    pl.when(jnp.logical_not(inside))(lambda: spread(t).start())

    def peer(r, m):
        ref = gat.at[r, :, c, p]
        return remote(ref, ref, p2_send.at[r, m], p2_recv.at[r, m], (c + m) % C * 2 + p, g)

    def forward(r, m):
        ref = gat.at[r, :, (c + C - m) % C, p]
        return remote(ref, ref, b_send.at[r, m], b_recv.at[r, m], sibling, g)

    def spread_in_plane(r):
        for h in range(NG):
            piece = gat.at[r, h, c, p]
            pltpu.make_async_copy(piece, piece, p1_recv.at[r, h]).wait()
        for m in range(1, C):
            peer(r, m).start()
        forward(r, 0).start()

    unit = 2.0 * math.pi / n
    kappa = scr_ref[0] * unit
    weight = -occ_ref[slot_ref[t]]
    signed = lambda i: jnp.where(i < n // 2, i, i - n).astype(f32) * unit
    lane = lax.broadcasted_iota(jnp.int32, (n, w), 1)
    gx = signed(lax.broadcasted_iota(jnp.int32, (n, w), 0))
    gz = signed(lane % n)
    base = gx * gx + gz * gz + kappa * kappa

    @pl.loop(0, n)
    def _(ky):
        gy = signed(ky)
        kern_ref[ky] = coulomb_scale / (base + gy * gy)

    load.wait()
    low = lax.broadcasted_iota(jnp.int32, (P2, w), 1) < n

    @pl.loop(0, C)
    def _(cc):
        for h in range(NG):
            q = partner[h, cc].astype(f32)
            turned = pltpu.roll(q, n, 1)
            q1_ref[h, cc] = jnp.where(low, q, turned).astype(bf16)
            q2_ref[h, cc] = jnp.where(low, -turned, q).astype(bf16)

    def dot(a, b):
        return jnp.dot(a, b, preferred_element_type=f32)

    def both(ref, h, cc):
        return jnp.concatenate([ref[h, cc], ref[h + 1, cc]], axis=0).astype(f32)

    def stage_one(r, cc):
        @pl.loop(0, NG // 2)
        def _(hh):
            h = hh * 2
            v = jnp.concatenate([gat[r, h, cc].reshape(P2, w), gat[r, h + 1, cc].reshape(P2, w)], axis=0).astype(f32)
            density = (both(q1_ref, h, cc) * v - both(q2_ref, h, cc) * pltpu.roll(v, n, 1)).astype(bf16)
            f = dot(density, fz_ref[...]).astype(bf16)
            for a in range(0, 2 * k, 2):
                stack = [
                    jnp.concatenate([f[b * n:(b + 1) * n, :w], f[b * n:(b + 1) * n, w:]], axis=0)
                    for b in (a, a + 1)
                ]
                o = dot(fy_ref[...], jnp.concatenate(stack, axis=1))
                for b in range(2):
                    x = ((h + (a + b) // k) * C + cc) * k + (a + b) % k
                    s1[pl.ds(x, w, stride=ld), :] = o[:, b * w:(b + 1) * w]

    def rows_of(s, i):
        top = s[pl.ds(pl.multiple_of(i * ld, 8), n), :]
        bottom = s[pl.ds(pl.multiple_of((i + n) * ld, 8), n), :]
        return jnp.concatenate([top, bottom], axis=0).astype(bf16)

    def stage_two():
        G = 8

        @pl.loop(0, n // G)
        def _(i):
            for a in range(0, G, 2):
                ky = i * G + a
                spectrum = dot(fy_ref[...], jnp.concatenate([rows_of(s1, ky), rows_of(s1, ky + 1)], axis=1))
                half = jnp.concatenate([kern_ref[ky], kern_ref[ky + 1]], axis=1)
                scaled = (spectrum * jnp.concatenate([half, half], axis=0)).astype(bf16)
                o = dot(iy_ref[...], scaled)
                for b in range(2):
                    s2[pl.ds(ky + b, w, stride=ld), :] = o[:, b * w:(b + 1) * w]

    def stage_three(r, cc):
        @pl.loop(0, NG // 2)
        def _(hh):
            h = hh * 2
            parts = []
            for a in range(0, 2 * k, 2):
                stack = [
                    rows_of(s2, ((h + e // k) * C + cc) * k + e % k) for e in (a, a + 1)
                ]
                o = dot(iy_ref[:n, :], jnp.concatenate(stack, axis=1)).astype(bf16)
                parts += [o[:, :w], o[:, w:]]
            potential = dot(jnp.concatenate(parts, axis=0), iz_ref[...])
            result = weight * (potential[:, :w] * both(q1_ref, h, cc) + potential[:, w:] * both(q2_ref, h, cc))
            result = result.astype(bf16)
            part[r, h, cc] = result[:P2].reshape(2, P2 // 2, w)
            part[r, h + 1, cc] = result[P2:].reshape(2, P2 // 2, w)

    def out_sibling(r, m):
        return remote(part.at[r, :, (c + m) % C, 1 - p], sib.at[r, m], s_send.at[r, m], s_recv.at[r, m], sibling, g)

    def out_peer(r, m):
        return remote(acc.at[r, m], inbox.at[r, m], r_send.at[r, m], r_recv.at[r, m], (c + m) % C * 2 + p, g)

    def to_owner(r, h):
        return remote(fin.at[r, h], final.at[t], f_send.at[r, h], f_recv.at[t], g * R + r, h)

    def add_sibling(r, m):
        out_sibling(r, m).wait_recv()
        mine = part[r, :, (c + m) % C, p]
        acc[r, m] = (mine.astype(f32) + sib[r, m].astype(f32)).astype(bf16)

    own_sum = pltpu.make_async_copy(fin.at[t % R, g], final.at[t], f_recv.at[t])

    def finish(r):
        for m in range(1, C):
            out_peer(r, m).wait_recv()
        total = acc[r, 0].astype(f32)
        for m in range(1, C):
            total = total + inbox[r, m].astype(f32)
        fin[r] = total.astype(bf16)
        for h in range(NG):
            here = (t == g * R + r) & (g == h)
            pl.when(here)(own_sum.start)
            pl.when(jnp.logical_not(here))(lambda: to_owner(r, h).start())

    spread_in_plane(0)
    for r in range(R):

        @pl.loop(1, C)
        def _(m):
            peer(r, m).wait_recv()
            forward(r, m).start()
            forward(r, m - 1).wait_recv()
            stage_one(r, (c + C - (m - 1)) % C)

        if r + 1 < R:
            spread_in_plane(r + 1)
        forward(r, C - 1).wait_recv()
        stage_one(r, (c + 1) % C)
        if r:
            finish(r - 1)
        stage_two()

        stage_three(r, (c + 1) % C)
        out_sibling(r, 1).start()

        @pl.loop(2, C)
        def _(m):
            stage_three(r, (c + m) % C)
            out_sibling(r, m).start()
            add_sibling(r, m - 1)
            out_peer(r, m - 1).start()

        stage_three(r, c)
        out_sibling(r, 0).start()
        add_sibling(r, C - 1)
        out_peer(r, C - 1).start()
        add_sibling(r, 0)
    finish(R - 1)

    for m in range(NT):
        j = (t + m) % NT
        piece = final.at[j]
        pltpu.make_async_copy(piece, piece, f_recv.at[j]).wait()
        out[j] = final[j].astype(f32)
    for m in range(1, NT):
        spread((t + m) % NT).wait_send()
    pl.when(jnp.logical_not(inside))(lambda: spread(t).wait_send())
    for r in range(R):
        for m in range(C):
            forward(r, m).wait_send()
            out_sibling(r, m).wait_send()
            if m:
                peer(r, m).wait_send()
                out_peer(r, m).wait_send()
        for h in range(NG):
            here = (t == g * R + r) & (g == h)
            pl.when(jnp.logical_not(here))(lambda: to_owner(r, h).wait_send())


def body(targets, partners, occupations, slot_partner, screening):
    NT, NG = lax.axis_size("tgt"), lax.axis_size("grp")
    R, C = NT // NG, NT // 2
    _, planes, n, w = targets.shape
    rows = planes * n // NT
    piece = (rows, w)
    anywhere = pl.BlockSpec(memory_space=pl.ANY)
    vmem = pl.BlockSpec(memory_space=pltpu.VMEM)
    smem = pl.BlockSpec(memory_space=pltpu.SMEM)
    dma = pltpu.SemaphoreType.DMA
    bf16, f32 = jnp.bfloat16, jnp.float32
    mats = [jnp.asarray(m) for m in matrices(n)]
    ld = n + 8
    field = (NG, C, 2 * rows, w)
    out = pl.pallas_call(
        functools.partial(exchange_kernel, NT, NG),
        out_shape=jax.ShapeDtypeStruct((NT,) + piece, f32),
        in_specs=[anywhere] * 2 + [vmem] * 4 + [smem] * 3,
        out_specs=vmem,
        scratch_shapes=[
            pltpu.VMEM((R, NG, C, 2) + piece, bf16),
            pltpu.VMEM(field, bf16),
            pltpu.VMEM(field, bf16),
            pltpu.VMEM(field, bf16),
            pltpu.VMEM((n, n, w), f32),
            pltpu.VMEM((w * ld, w), f32),
            pltpu.VMEM((w * ld, w), f32),
            pltpu.VMEM((R, NG, C, 2) + piece, bf16),
            pltpu.VMEM((R, C, NG) + piece, bf16),
            pltpu.VMEM((R, C, NG) + piece, bf16),
            pltpu.VMEM((R, C, NG) + piece, bf16),
            pltpu.VMEM((R, NG) + piece, bf16),
            pltpu.VMEM((NT,) + piece, bf16),
            dma, dma((NT,)), dma((R, NG)), dma((R, C)), dma((R, C)), dma((R, C)), dma((R, C)),
            dma((R, C)), dma((R, C)), dma((R, C)), dma((R, C)), dma((R, NG)), dma((NT,)),
        ],
        compiler_params=pltpu.CompilerParams(
            collective_id=0, has_side_effects=True, vmem_limit_bytes=52 << 20),
    )(targets.reshape((NT,) + piece), partners.reshape(field), *mats, occupations, slot_partner, screening)
    return out.reshape(targets.shape)


def solution(mesh):
    in_specs = (P("tgt", "grp", None, None), P("tgt", None, None, None), P(), P(), P())
    out_specs = P("tgt", "grp", None, None)
    return jax.shard_map(body, mesh=mesh, in_specs=in_specs, out_specs=out_specs, check_vma=False)
```

time: 168 us -> 74.4 us (0.44)
  waiting for transfers between devices: 85.3 us -> 0 us
  Pallas kernels: 0 us -> 67.8 us
  other arithmetic: 38.7 us -> 0 us
  matrix products: 17.1 us -> 0 us
  between operations: 14.3 us -> 0.68 us
  starting transfers between devices: 5.44 us -> 0 us
    pallas_call x0 -> x1, Pallas kernels: none -> 67.8 us  [body(): pl.pallas_call(functools.partial(exchange_kernel, NT, NG), out_shape=jax....]
    ppermute x3 -> x0, waiting for transfers between devices: 53.9 us -> none  [from_behind(): return lax.ppermute(value, axis, pairs)]
    reduce_scatter x1 -> x0, waiting for transfers between devices: 30.1 us -> none  [body(): lax.psum_scatter(totals.astype(jnp.bfloat16), 'grp', scatter_dimension=1,...]
    concatenate x16 -> x0, other arithmetic: 27 us -> none  [the longest x14 21.5 us: combine(): return jnp.concatenate([real_part, imag_part], axis=-1).astype(jnp.bfloat16)]
    dot_general x10 -> x0, matrix products: 17.1 us -> none  [the longest x4 11.1 us: section_middle(): jnp.einsum('ky,bxyw->bxkw', tables, field, preferred_element_type=jnp.flo...]
    ppermute x3 -> x0, starting transfers between devices: 5.39 us -> none  [from_behind(): return lax.ppermute(value, axis, pairs)]
    unnamed x8 -> x15, local copies, waits for them, and re-layouts: 0.46 us -> 5.59 us
    dot_general x2 -> x0, local copies, waits for them, and re-layouts: 5.12 us -> none  [section_middle(): jnp.einsum('ky,bxyw->bxkw', tables, field, preferred_element_type=jnp.flo...]
  transfers between devices with their start and end apart: 5 -> 0, of which waited for: 5 -> 0; matrix products, arithmetic and copies ran while one was open for 1% -> 0% of each run, Pallas kernels for 0% -> 0%
where the time goes in v2:
time: 74.4 us; the launch traced here: 74 us
  Pallas kernels  67.8 us (91%)
  local copies, waits for them, and re-layouts  5.59 us (8%)
    pallas_call x1, Pallas kernels, body(): pl.pallas_call(functools.partial(exchange_kernel, NT, NG), out_shape=jax....  67.8 us
    unnamed x15, local copies, waits for them, and re-layouts  5.59 us

profile of v2, /device:TPU:1, one launch (start us, length us, event | category | flops | bytes accessed | tf_op | source)
XLA Modules:
  0.0 74.0 jit_solution(3157907066632856679)
XLA Ops:
  0.7 0.0 copy-start.5
  0.7 0.0 copy-start.6
  0.7 0.6 copy-done.5
  1.3 0.0 copy-done.6
  1.3 0.0 copy-start
  1.3 0.9 %copy-done = bf16[1,16,64,128]{3,2,1,0:T(8,128)(2,1)S(1)} copy-done((bf16[1,16,64,128]{3,2,1,0:T(8,128)(2,1)S(1)}, bf16[1,16,64,128]{3,2,1,0:T(8,128)(2,1)}, u32[]{:S(2)}) %copy-start) | copy-done | bytes 262168
  2.3 0.0 copy-start.1
  2.3 0.8 %copy-done.1 = bf16[128,256]{1,0:T(8,128)(2,1)S(1)} copy-done((bf16[128,256]{1,0:T(8,128)(2,1)S(1)}, bf16[128,256]{1,0:T(8,128)(2,1)}, u32[]{:S(2)}) %copy-start.1) | copy-done | bytes 65560
  3.1 0.0 copy-start.2
  3.1 0.8 %copy-done.2 = bf16[128,256]{1,0:T(8,128)(2,1)S(1)} copy-done((bf16[128,256]{1,0:T(8,128)(2,1)S(1)}, bf16[128,256]{1,0:T(8,128)(2,1)}, u32[]{:S(2)}) %copy-start.2) | copy-done | bytes 65560
  4.0 0.0 copy-start.3
  4.0 0.8 %copy-done.3 = bf16[128,128]{1,0:T(8,128)(2,1)S(1)} copy-done((bf16[128,128]{1,0:T(8,128)(2,1)S(1)}, bf16[128,128]{1,0:T(8,128)(2,1)}, u32[]{:S(2)}) %copy-start.3) | copy-done | bytes 32792
  4.7 0.0 copy-start.4
  4.7 0.8 %copy-done.4 = bf16[128,128]{1,0:T(8,128)(2,1)S(1)} copy-done((bf16[128,128]{1,0:T(8,128)(2,1)S(1)}, bf16[128,128]{1,0:T(8,128)(2,1)}, u32[]{:S(2)}) %copy-start.4) | copy-done | bytes 32792
  5.5 67.8 %shard_map.91 = f32[8,128,128]{2,1,0:T(8,128)S(1)} custom-call(bf16[8,128,128]{2,1,0:T(8,128)(2,1)S(1)} %bitcast.4, bf16[4,4,256,128]{3,2,1,0:T(8,128)(2,1)} %bitcast.5, bf16[128,256]{1,0:T(8,128)(2,1)S(1)} %copy-done.2, bf16[128,128]{1,0:T(8,128)(2,1)S(1)} %copy-done.4, bf16[128,128]{1,0:T(8,128)(2,1)S(1)} %copy-done.3, bf16[128,256]{1,0:T(8,128)(2,1)S(1)} %copy-done.1, ...), custom_call_target="tpu_custom_call" | custom-call | tf_op jit(solution)/shard_map/pallas_call | solution.py:292
  73.2 0.8 %copy.12 = f32[1,16,64,128]{3,2,1,0:T(8,128)} copy(f32[1,16,64,128]{3,2,1,0:T(8,128)S(1)} %bitcast.3) | data formatting | bytes 1048576
Async XLA Ops:
  0.7 0.7 copy-start.5
  0.7 0.7 copy-start.6
  1.3 0.9 %copy-start = (bf16[1,16,64,128]{3,2,1,0:T(8,128)(2,1)S(1)}, bf16[1,16,64,128]{3,2,1,0:T(8,128)(2,1)}, u32[]{:S(2)}) copy-start(bf16[1,16,64,128]{3,2,1,0:T(8,128)(2,1)} %param.9) | copy-start | bytes 786436
  2.3 0.8 %copy-start.1 = (bf16[128,256]{1,0:T(8,128)(2,1)S(1)}, bf16[128,256]{1,0:T(8,128)(2,1)}, u32[]{:S(2)}) copy-start(bf16[128,256]{1,0:T(8,128)(2,1)} %constant.11.clone.iz_ref) | copy-start | bytes 196612
  3.1 0.8 %copy-start.2 = (bf16[128,256]{1,0:T(8,128)(2,1)S(1)}, bf16[128,256]{1,0:T(8,128)(2,1)}, u32[]{:S(2)}) copy-start(bf16[128,256]{1,0:T(8,128)(2,1)} %constant.8.clone.fz_ref) | copy-start | bytes 196612
  4.0 0.8 %copy-start.3 = (bf16[128,128]{1,0:T(8,128)(2,1)S(1)}, bf16[128,128]{1,0:T(8,128)(2,1)}, u32[]{:S(2)}) copy-start(bf16[128,128]{1,0:T(8,128)(2,1)} %constant.10.clone.iy_ref) | copy-start | bytes 98308
  4.7 0.8 %copy-start.4 = (bf16[128,128]{1,0:T(8,128)(2,1)S(1)}, bf16[128,128]{1,0:T(8,128)(2,1)}, u32[]{:S(2)}) copy-start(bf16[128,128]{1,0:T(8,128)(2,1)} %constant.9.clone.fy_ref) | copy-start | bytes 98308

commit v3 on v2

--- a/solution.py
+++ b/solution.py
@@ -58,26 +58,18 @@
     def greet(*device):
         pl.semaphore_signal(barrier, inc=1, device_id=device, device_id_type=MESH)
 
-    for m in range(NT):
-        if m == 0:
-            pl.when(jnp.logical_not(inside))(lambda: greet(t, own_set))
-        else:
-            greet((t + m) % NT, own_set)
     for r in range(R):
         for h in range(NG):
             here = (t == g * R + r) & (g == h)
             pl.when(jnp.logical_not(here))(lambda: greet(g * R + r, h))
-    for m in range(1, C):
-        greet((c + m) % C * 2 + p, g)
-    greet(sibling, g)
 
     @pl.when(inside)
     def _():
-        pl.semaphore_wait(barrier, 2 * NT - 2 + C)
+        pl.semaphore_wait(barrier, NT - 1)
 
     @pl.when(jnp.logical_not(inside))
     def _():
-        pl.semaphore_wait(barrier, 2 * NT + C)
+        pl.semaphore_wait(barrier, NT)
 
     def remote(a, b, send, recv, *device):
         return pltpu.make_async_remote_copy(
@@ -92,20 +84,24 @@
     pl.when(inside)(own_piece.start)
     pl.when(jnp.logical_not(inside))(lambda: spread(t).start())
 
-    def peer(r, m):
-        ref = gat.at[r, :, c, p]
-        return remote(ref, ref, p2_send.at[r, m], p2_recv.at[r, m], (c + m) % C * 2 + p, g)
+    def peer(r, m, h):
+        ref = gat.at[r, h, c, p]
+        return remote(ref, ref, p2_send.at[r, m, h], p2_recv.at[r, m, h], (c + m) % C * 2 + p, g)
 
     def forward(r, m):
         ref = gat.at[r, :, (c + C - m) % C, p]
         return remote(ref, ref, b_send.at[r, m], b_recv.at[r, m], sibling, g)
 
     def spread_in_plane(r):
-        for h in range(NG):
+        for d in (0, 1, NG - 1, *range(2, NG - 1)):
+            h = (g + d) % NG
             piece = gat.at[r, h, c, p]
             pltpu.make_async_copy(piece, piece, p1_recv.at[r, h]).wait()
-        for m in range(1, C):
-            peer(r, m).start()
+
+            @pl.loop(1, C)
+            def _(m):
+                peer(r, m, h).start()
+
         forward(r, 0).start()
 
     unit = 2.0 * math.pi / n
@@ -116,11 +112,6 @@
     gx = signed(lax.broadcasted_iota(jnp.int32, (n, w), 0))
     gz = signed(lane % n)
     base = gx * gx + gz * gz + kappa * kappa
-
-    @pl.loop(0, n)
-    def _(ky):
-        gy = signed(ky)
-        kern_ref[ky] = coulomb_scale / (base + gy * gy)
 
     load.wait()
     low = lax.broadcasted_iota(jnp.int32, (P2, w), 1) < n
@@ -195,8 +186,13 @@
     def out_sibling(r, m):
         return remote(part.at[r, :, (c + m) % C, 1 - p], sib.at[r, m], s_send.at[r, m], s_recv.at[r, m], sibling, g)
 
-    def out_peer(r, m):
-        return remote(acc.at[r, m], inbox.at[r, m], r_send.at[r, m], r_recv.at[r, m], (c + m) % C * 2 + p, g)
+    def out_peer(r, m, h):
+        return remote(acc.at[r, m, h], inbox.at[r, m, h], r_send.at[r, m, h], r_recv.at[r, m, h],
+                      (c + m) % C * 2 + p, g)
+
+    def send_peer(r, m):
+        for d in range(1, NG + 1):
+            out_peer(r, m, (g + d) % NG).start()
 
     def to_owner(r, h):
         return remote(fin.at[r, h], final.at[t], f_send.at[r, h], f_recv.at[t], g * R + r, h)
@@ -209,29 +205,35 @@
     own_sum = pltpu.make_async_copy(fin.at[t % R, g], final.at[t], f_recv.at[t])
 
     def finish(r):
-        for m in range(1, C):
-            out_peer(r, m).wait_recv()
-        total = acc[r, 0].astype(f32)
-        for m in range(1, C):
-            total = total + inbox[r, m].astype(f32)
-        fin[r] = total.astype(bf16)
-        for h in range(NG):
+        for d in range(1, NG + 1):
+            h = (g + d) % NG
+            total = acc[r, 0, h].astype(f32)
+            for m in range(1, C):
+                out_peer(r, m, h).wait_recv()
+                total = total + inbox[r, m, h].astype(f32)
+            fin[r, h] = total.astype(bf16)
             here = (t == g * R + r) & (g == h)
             pl.when(here)(own_sum.start)
             pl.when(jnp.logical_not(here))(lambda: to_owner(r, h).start())
 
-    spread_in_plane(0)
+    for r in range(R):
+        spread_in_plane(r)
+
+    @pl.loop(0, n)
+    def _(ky):
+        gy = signed(ky)
+        kern_ref[ky] = coulomb_scale / (base + gy * gy)
+
     for r in range(R):
 
         @pl.loop(1, C)
         def _(m):
-            peer(r, m).wait_recv()
+            for h in range(NG):
+                peer(r, m, h).wait_recv()
             forward(r, m).start()
             forward(r, m - 1).wait_recv()
             stage_one(r, (c + C - (m - 1)) % C)
 
-        if r + 1 < R:
-            spread_in_plane(r + 1)
         forward(r, C - 1).wait_recv()
         stage_one(r, (c + 1) % C)
         if r:
@@ -246,12 +248,12 @@
             stage_three(r, (c + m) % C)
             out_sibling(r, m).start()
             add_sibling(r, m - 1)
-            out_peer(r, m - 1).start()
+            send_peer(r, m - 1)
 
         stage_three(r, c)
         out_sibling(r, 0).start()
         add_sibling(r, C - 1)
-        out_peer(r, C - 1).start()
+        send_peer(r, C - 1)
         add_sibling(r, 0)
     finish(R - 1)
 
@@ -267,9 +269,9 @@
         for m in range(C):
             forward(r, m).wait_send()
             out_sibling(r, m).wait_send()
-            if m:
-                peer(r, m).wait_send()
-                out_peer(r, m).wait_send()
+            for h in range(NG if m else 0):
+                peer(r, m, h).wait_send()
+                out_peer(r, m, h).wait_send()
         for h in range(NG):
             here = (t == g * R + r) & (g == h)
             pl.when(jnp.logical_not(here))(lambda: to_owner(r, h).wait_send())
@@ -308,8 +310,8 @@
             pltpu.VMEM((R, C, NG) + piece, bf16),
             pltpu.VMEM((R, NG) + piece, bf16),
             pltpu.VMEM((NT,) + piece, bf16),
-            dma, dma((NT,)), dma((R, NG)), dma((R, C)), dma((R, C)), dma((R, C)), dma((R, C)),
-            dma((R, C)), dma((R, C)), dma((R, C)), dma((R, C)), dma((R, NG)), dma((NT,)),
+            dma, dma((NT,)), dma((R, NG)), dma((R, C, NG)), dma((R, C, NG)), dma((R, C)), dma((R, C)),
+            dma((R, C)), dma((R, C)), dma((R, C, NG)), dma((R, C, NG)), dma((R, NG)), dma((NT,)),
         ],
         compiler_params=pltpu.CompilerParams(
             collective_id=0, has_side_effects=True, vmem_limit_bytes=52 << 20),

time: 74.4 us -> 75.1 us (level)
  no operation moved by 1% of the time
where the time goes in v3:
time: 75.1 us; the launch traced here: 74.7 us
  Pallas kernels  68.5 us (91%)
  local copies, waits for them, and re-layouts  5.59 us (7%)
    pallas_call x1, Pallas kernels, body(): pl.pallas_call(functools.partial(exchange_kernel, NT, NG), out_shape=jax....  68.5 us
    unnamed x15, local copies, waits for them, and re-layouts  5.59 us

profile of v3, /device:TPU:1, one launch (start us, length us, event | category | flops | bytes accessed | tf_op | source)
XLA Modules:
  0.0 74.7 jit_solution(2878028142244498863)
XLA Ops:
  0.7 0.0 copy-start.5
  0.7 0.0 copy-start.6
  0.7 0.6 copy-done.5
  1.3 0.0 copy-done.6
  1.3 0.0 copy-start
  1.3 0.9 %copy-done = bf16[1,16,64,128]{3,2,1,0:T(8,128)(2,1)S(1)} copy-done((bf16[1,16,64,128]{3,2,1,0:T(8,128)(2,1)S(1)}, bf16[1,16,64,128]{3,2,1,0:T(8,128)(2,1)}, u32[]{:S(2)}) %copy-start) | copy-done | bytes 262168
  2.3 0.0 copy-start.1
  2.3 0.8 %copy-done.1 = bf16[128,256]{1,0:T(8,128)(2,1)S(1)} copy-done((bf16[128,256]{1,0:T(8,128)(2,1)S(1)}, bf16[128,256]{1,0:T(8,128)(2,1)}, u32[]{:S(2)}) %copy-start.1) | copy-done | bytes 65560
  3.1 0.0 copy-start.2
  3.1 0.8 %copy-done.2 = bf16[128,256]{1,0:T(8,128)(2,1)S(1)} copy-done((bf16[128,256]{1,0:T(8,128)(2,1)S(1)}, bf16[128,256]{1,0:T(8,128)(2,1)}, u32[]{:S(2)}) %copy-start.2) | copy-done | bytes 65560
  4.0 0.0 copy-start.3
  4.0 0.8 %copy-done.3 = bf16[128,128]{1,0:T(8,128)(2,1)S(1)} copy-done((bf16[128,128]{1,0:T(8,128)(2,1)S(1)}, bf16[128,128]{1,0:T(8,128)(2,1)}, u32[]{:S(2)}) %copy-start.3) | copy-done | bytes 32792
  4.7 0.0 copy-start.4
  4.7 0.8 %copy-done.4 = bf16[128,128]{1,0:T(8,128)(2,1)S(1)} copy-done((bf16[128,128]{1,0:T(8,128)(2,1)S(1)}, bf16[128,128]{1,0:T(8,128)(2,1)}, u32[]{:S(2)}) %copy-start.4) | copy-done | bytes 32792
  5.5 68.5 %shard_map.91 = f32[8,128,128]{2,1,0:T(8,128)S(1)} custom-call(bf16[8,128,128]{2,1,0:T(8,128)(2,1)S(1)} %bitcast.4, bf16[4,4,256,128]{3,2,1,0:T(8,128)(2,1)} %bitcast.5, bf16[128,256]{1,0:T(8,128)(2,1)S(1)} %copy-done.2, bf16[128,128]{1,0:T(8,128)(2,1)S(1)} %copy-done.4, bf16[128,128]{1,0:T(8,128)(2,1)S(1)} %copy-done.3, bf16[128,256]{1,0:T(8,128)(2,1)S(1)} %copy-done.1, ...), custom_call_target="tpu_custom_call" | custom-call | tf_op jit(solution)/shard_map/pallas_call | solution.py:294
  73.9 0.8 %copy.12 = f32[1,16,64,128]{3,2,1,0:T(8,128)} copy(f32[1,16,64,128]{3,2,1,0:T(8,128)S(1)} %bitcast.3) | data formatting | bytes 1048576
Async XLA Ops:
  0.7 0.7 copy-start.5
  0.7 0.7 copy-start.6
  1.3 0.9 %copy-start = (bf16[1,16,64,128]{3,2,1,0:T(8,128)(2,1)S(1)}, bf16[1,16,64,128]{3,2,1,0:T(8,128)(2,1)}, u32[]{:S(2)}) copy-start(bf16[1,16,64,128]{3,2,1,0:T(8,128)(2,1)} %param.9) | copy-start | bytes 786436
  2.3 0.8 %copy-start.1 = (bf16[128,256]{1,0:T(8,128)(2,1)S(1)}, bf16[128,256]{1,0:T(8,128)(2,1)}, u32[]{:S(2)}) copy-start(bf16[128,256]{1,0:T(8,128)(2,1)} %constant.11.clone.iz_ref) | copy-start | bytes 196612
  3.1 0.8 %copy-start.2 = (bf16[128,256]{1,0:T(8,128)(2,1)S(1)}, bf16[128,256]{1,0:T(8,128)(2,1)}, u32[]{:S(2)}) copy-start(bf16[128,256]{1,0:T(8,128)(2,1)} %constant.8.clone.fz_ref) | copy-start | bytes 196612
  4.0 0.8 %copy-start.3 = (bf16[128,128]{1,0:T(8,128)(2,1)S(1)}, bf16[128,128]{1,0:T(8,128)(2,1)}, u32[]{:S(2)}) copy-start(bf16[128,128]{1,0:T(8,128)(2,1)} %constant.10.clone.iy_ref) | copy-start | bytes 98308
  4.7 0.8 %copy-start.4 = (bf16[128,128]{1,0:T(8,128)(2,1)S(1)}, bf16[128,128]{1,0:T(8,128)(2,1)}, u32[]{:S(2)}) copy-start(bf16[128,128]{1,0:T(8,128)(2,1)} %constant.9.clone.fy_ref) | copy-start | bytes 98308

commit v4 on v3

--- a/solution.py
+++ b/solution.py
@@ -34,8 +34,8 @@
 
 
 def exchange_kernel(NT, NG, src, part_hbm, fz_ref, fy_ref, iy_ref, iz_ref, occ_ref, slot_ref, scr_ref, out,
-                    gat, partner, q1_ref, q2_ref, kern_ref, s1, s2, part, sib, acc, inbox, fin, final,
-                    load_sem, p1_send, p1_recv, p2_send, p2_recv, b_send, b_recv,
+                    mid, gat, partner, q1_ref, q2_ref, kern_ref, s1, s2, part, sib, acc, inbox, fin, final,
+                    load_sem, p0_send, p0_recv, p1_send, p1_recv, p2_send, p2_recv, b_send, b_recv,
                     s_send, s_recv, r_send, r_recv, f_send, f_recv):
     f32, bf16 = jnp.float32, jnp.bfloat16
     R, C = NT // NG, NT // 2
@@ -46,9 +46,7 @@
     ld = s1.shape[0] // w
     t, g = lax.axis_index("tgt"), lax.axis_index("grp")
     c, p = t // 2, t % 2
-    own_set = t // R
     sibling = c * 2 + 1 - p
-    inside = own_set == g
 
     load = pltpu.make_async_copy(part_hbm, partner, load_sem)
     load.start()
@@ -58,31 +56,34 @@
     def greet(*device):
         pl.semaphore_signal(barrier, inc=1, device_id=device, device_id_type=MESH)
 
-    for r in range(R):
-        for h in range(NG):
-            here = (t == g * R + r) & (g == h)
-            pl.when(jnp.logical_not(here))(lambda: greet(g * R + r, h))
-
-    @pl.when(inside)
-    def _():
-        pl.semaphore_wait(barrier, NT - 1)
-
-    @pl.when(jnp.logical_not(inside))
-    def _():
-        pl.semaphore_wait(barrier, NT)
+    for m in range(1, NT):
+        greet((t + m) % NT, g)
+    for d in range(1, NG):
+        greet(t, (g + d) % NG)
+    pl.semaphore_wait(barrier, NT + NG - 2)
 
     def remote(a, b, send, recv, *device):
         return pltpu.make_async_remote_copy(
             src_ref=a, dst_ref=b, send_sem=send, recv_sem=recv, device_id=device, device_id_type=MESH)
 
     def spread(j):
-        return remote(src.at[j], gat.at[t % R, g, j // 2, j % 2], p1_send.at[j], p1_recv.at[t % R, g], j, own_set)
-
-    own_piece = pltpu.make_async_copy(src.at[t], gat.at[t % R, g, c, p], p1_recv.at[t % R, g])
+        return remote(src.at[j], mid.at[t], p0_send.at[j], p0_recv.at[t], j, g)
+
+    def along(h, r):
+        return remote(mid.at[h * R + r], gat.at[r, g, c, p], p1_send.at[h, r], p1_recv.at[r, g], t, h)
+
+    own_piece = pltpu.make_async_copy(src.at[t], mid.at[t], p0_recv.at[t])
     for m in range(1, NT):
         spread((t + m) % NT).start()
-    pl.when(inside)(own_piece.start)
-    pl.when(jnp.logical_not(inside))(lambda: spread(t).start())
+    own_piece.start()
+    for d in (*range(1, NG), 0):
+        h = (g + d) % NG
+        for r in range(R):
+            pltpu.make_async_copy(mid.at[h * R + r], mid.at[h * R + r], p0_recv.at[h * R + r]).wait()
+            if d:
+                along(h, r).start()
+            else:
+                pltpu.make_async_copy(mid.at[g * R + r], gat.at[r, g, c, p], p1_recv.at[r, g]).start()
 
     def peer(r, m, h):
         ref = gat.at[r, h, c, p]
@@ -264,7 +265,9 @@
         out[j] = final[j].astype(f32)
     for m in range(1, NT):
         spread((t + m) % NT).wait_send()
-    pl.when(jnp.logical_not(inside))(lambda: spread(t).wait_send())
+    for d in range(1, NG):
+        for r in range(R):
+            along((g + d) % NG, r).wait_send()
     for r in range(R):
         for m in range(C):
             forward(r, m).wait_send()
@@ -297,6 +300,7 @@
         in_specs=[anywhere] * 2 + [vmem] * 4 + [smem] * 3,
         out_specs=vmem,
         scratch_shapes=[
+            pltpu.VMEM((NT,) + piece, bf16),
             pltpu.VMEM((R, NG, C, 2) + piece, bf16),
             pltpu.VMEM(field, bf16),
             pltpu.VMEM(field, bf16),
@@ -310,7 +314,7 @@
             pltpu.VMEM((R, C, NG) + piece, bf16),
             pltpu.VMEM((R, NG) + piece, bf16),
             pltpu.VMEM((NT,) + piece, bf16),
-            dma, dma((NT,)), dma((R, NG)), dma((R, C, NG)), dma((R, C, NG)), dma((R, C)), dma((R, C)),
+            dma, dma((NT,)), dma((NT,)), dma((NG, R)), dma((R, NG)), dma((R, C, NG)), dma((R, C, NG)), dma((R, C)), dma((R, C)),
             dma((R, C)), dma((R, C)), dma((R, C, NG)), dma((R, C, NG)), dma((R, NG)), dma((NT,)),
         ],
         compiler_params=pltpu.CompilerParams(

time: 75.1 us -> 65.8 us (0.88); the launches traced: 74.7 us -> 64.5 us
  Pallas kernels: 68.5 us -> 58.2 us
    pallas_call x1, Pallas kernels: 68.5 us -> 58.2 us  [body(): pl.pallas_call(functools.partial(exchange_kernel, NT, NG), out_shape=jax....]
where the time goes in v4:
time: 65.8 us; the launch traced here: 64.5 us
  Pallas kernels  58.2 us (88%)
  local copies, waits for them, and re-layouts  5.59 us (8%)
  between operations  0.68 us (1%)
    pallas_call x1, Pallas kernels, body(): pl.pallas_call(functools.partial(exchange_kernel, NT, NG), out_shape=jax....  58.2 us
    unnamed x15, local copies, waits for them, and re-layouts  5.59 us

profile of v4, /device:TPU:1, one launch (start us, length us, event | category | flops | bytes accessed | tf_op | source)
XLA Modules:
  0.0 64.5 jit_solution(5603389168032946154)
XLA Ops:
  0.7 0.0 copy-start.5
  0.7 0.0 copy-start.6
  0.7 0.6 copy-done.5
  1.3 0.0 copy-done.6
  1.3 0.0 copy-start
  1.3 0.9 %copy-done = bf16[1,16,64,128]{3,2,1,0:T(8,128)(2,1)S(1)} copy-done((bf16[1,16,64,128]{3,2,1,0:T(8,128)(2,1)S(1)}, bf16[1,16,64,128]{3,2,1,0:T(8,128)(2,1)}, u32[]{:S(2)}) %copy-start) | copy-done | bytes 262168
  2.3 0.0 copy-start.1
  2.3 0.8 %copy-done.1 = bf16[128,256]{1,0:T(8,128)(2,1)S(1)} copy-done((bf16[128,256]{1,0:T(8,128)(2,1)S(1)}, bf16[128,256]{1,0:T(8,128)(2,1)}, u32[]{:S(2)}) %copy-start.1) | copy-done | bytes 65560
  3.1 0.0 copy-start.2
  3.1 0.8 %copy-done.2 = bf16[128,256]{1,0:T(8,128)(2,1)S(1)} copy-done((bf16[128,256]{1,0:T(8,128)(2,1)S(1)}, bf16[128,256]{1,0:T(8,128)(2,1)}, u32[]{:S(2)}) %copy-start.2) | copy-done | bytes 65560
  4.0 0.0 copy-start.3
  4.0 0.8 %copy-done.3 = bf16[128,128]{1,0:T(8,128)(2,1)S(1)} copy-done((bf16[128,128]{1,0:T(8,128)(2,1)S(1)}, bf16[128,128]{1,0:T(8,128)(2,1)}, u32[]{:S(2)}) %copy-start.3) | copy-done | bytes 32792
  4.7 0.0 copy-start.4
  4.7 0.8 %copy-done.4 = bf16[128,128]{1,0:T(8,128)(2,1)S(1)} copy-done((bf16[128,128]{1,0:T(8,128)(2,1)S(1)}, bf16[128,128]{1,0:T(8,128)(2,1)}, u32[]{:S(2)}) %copy-start.4) | copy-done | bytes 32792
  5.5 58.2 %shard_map.91 = f32[8,128,128]{2,1,0:T(8,128)S(1)} custom-call(bf16[8,128,128]{2,1,0:T(8,128)(2,1)S(1)} %bitcast.4, bf16[4,4,256,128]{3,2,1,0:T(8,128)(2,1)} %bitcast.5, bf16[128,256]{1,0:T(8,128)(2,1)S(1)} %copy-done.2, bf16[128,128]{1,0:T(8,128)(2,1)S(1)} %copy-done.4, bf16[128,128]{1,0:T(8,128)(2,1)S(1)} %copy-done.3, bf16[128,256]{1,0:T(8,128)(2,1)S(1)} %copy-done.1, ...), custom_call_target="tpu_custom_call" | custom-call | tf_op jit(solution)/shard_map/pallas_call | solution.py:297
  63.7 0.8 %copy.12 = f32[1,16,64,128]{3,2,1,0:T(8,128)} copy(f32[1,16,64,128]{3,2,1,0:T(8,128)S(1)} %bitcast.3) | data formatting | bytes 1048576
Async XLA Ops:
  0.7 0.7 %copy-start.5 = (f32[8]{0:T(128)S(1)}, f32[8]{0:T(128)}, u32[]{:S(2)}) copy-start(f32[8]{0:T(128)} %occ_ref.1) | copy-start | bytes 100
  0.7 0.7 %copy-start.6 = (s32[8]{0:T(128)S(1)}, s32[8]{0:T(128)}, u32[]{:S(2)}) copy-start(s32[8]{0:T(128)} %slot_ref.1) | copy-start | bytes 100
  1.3 0.9 %copy-start = (bf16[1,16,64,128]{3,2,1,0:T(8,128)(2,1)S(1)}, bf16[1,16,64,128]{3,2,1,0:T(8,128)(2,1)}, u32[]{:S(2)}) copy-start(bf16[1,16,64,128]{3,2,1,0:T(8,128)(2,1)} %param.9) | copy-start | bytes 786436
  2.3 0.8 %copy-start.1 = (bf16[128,256]{1,0:T(8,128)(2,1)S(1)}, bf16[128,256]{1,0:T(8,128)(2,1)}, u32[]{:S(2)}) copy-start(bf16[128,256]{1,0:T(8,128)(2,1)} %constant.11.clone.iz_ref) | copy-start | bytes 196612
  3.1 0.8 %copy-start.2 = (bf16[128,256]{1,0:T(8,128)(2,1)S(1)}, bf16[128,256]{1,0:T(8,128)(2,1)}, u32[]{:S(2)}) copy-start(bf16[128,256]{1,0:T(8,128)(2,1)} %constant.8.clone.fz_ref) | copy-start | bytes 196612
  4.0 0.8 %copy-start.3 = (bf16[128,128]{1,0:T(8,128)(2,1)S(1)}, bf16[128,128]{1,0:T(8,128)(2,1)}, u32[]{:S(2)}) copy-start(bf16[128,128]{1,0:T(8,128)(2,1)} %constant.10.clone.iy_ref) | copy-start | bytes 98308
  4.7 0.8 %copy-start.4 = (bf16[128,128]{1,0:T(8,128)(2,1)S(1)}, bf16[128,128]{1,0:T(8,128)(2,1)}, u32[]{:S(2)}) copy-start(bf16[128,128]{1,0:T(8,128)(2,1)} %constant.9.clone.fy_ref) | copy-start | bytes 98308
